TPU v7x, 512 devices: a whole 4x4x16 slice. The times are simulated.
512 devices in a mesh: head: 8 (over x, core), tok: 64 (over z, y).
Axes of the slice: x: 4, y: 4, z: 16, core: 2. Of those that a mesh axis runs over, the one named last changes fastest.
Arguments:
- query_one: bfloat16 [16384, 4096], P(('head', 'tok')), may hold values from -6 to 6
- key_one: bfloat16 [16384, 4096], P(('head', 'tok')), may hold values from -6 to 6
- value_one: bfloat16 [16384, 4096], P(('head', 'tok')), may hold values from -6 to 6
- rate_one: bfloat16 [16384, 8], P(('head', 'tok')), may hold values from 0.099609375 to 1
- query_two: bfloat16 [16384, 4096], P(('head', 'tok')), may hold values from -6 to 6
- w_gate: float32 [8, 512, 512], P('head', 'tok'), may hold values from -0.25 to 0.25
- w_up: float32 [8, 512, 512], P('head', 'tok'), may hold values from -0.25 to 0.25
- w_down: float32 [8, 512, 512], P('head', 'tok'), may hold values from -0.25 to 0.25
- step_size: float32 [8], P('head'), may hold values from 0.02 to 0.08
Outputs:
- out_one: bfloat16 [16384, 4096], P(('head', 'tok'))
- out_two: bfloat16 [16384, 4096], P(('head', 'tok'))
- gate_new: float32 [8, 512, 512], P('head', 'tok')
- up_new: float32 [8, 512, 512], P('head', 'tok')
- down_new: float32 [8, 512, 512], P('head', 'tok')
All inputs are finite; a program needn't handle non-finite values.
Results may differ from a plain program's by a relative error of at most 0.011.
Values may be sent and summed in bfloat16 or wider, within the bound.
A program may use at most 64 MiB of HBM per device.

v0:
```python
import jax
import jax.numpy as jnp
from jax import lax
from jax.sharding import PartitionSpec as P


def apply_piece(query, gate_b, up_b, down_b):
    pre_gate = jnp.einsum("thd,hjd->htj", query, gate_b, preferred_element_type=jnp.float32)
    pre_up = jnp.einsum("thd,hjd->htj", query, up_b, preferred_element_type=jnp.float32)
    hidden = (pre_gate * jax.nn.sigmoid(pre_gate) * pre_up).astype(jnp.bfloat16)
    return jnp.einsum("htj,hjd->thd", hidden, down_b, preferred_element_type=jnp.float32)


def forward_piece(query, keys, targets, gate_b, up_b, down_b):
    out_term = apply_piece(query, gate_b, up_b, down_b)
    key_gate = jnp.einsum("thd,hjd->htj", keys, gate_b, preferred_element_type=jnp.float32)
    key_up = jnp.einsum("thd,hjd->htj", keys, up_b, preferred_element_type=jnp.float32)
    sigmoid_k = jax.nn.sigmoid(key_gate)
    act_k = key_gate * sigmoid_k
    hidden_k = (act_k * key_up).astype(jnp.bfloat16)
    back = jnp.einsum("thd,hjd->htj", targets, down_b, preferred_element_type=jnp.float32)
    grad_gate_pre = (back * key_up * sigmoid_k * (1.0 + key_gate * (1.0 - sigmoid_k))).astype(
        jnp.bfloat16
    )
    grad_up_pre = (back * act_k).astype(jnp.bfloat16)
    return (out_term, grad_gate_pre, grad_up_pre, hidden_k)


def gradient_rows(gate_all, up_all, hidden_all, keys, targets):
    grad_gate = jnp.einsum("htj,thd->jhd", gate_all, keys, preferred_element_type=jnp.float32)
    grad_up = jnp.einsum("htj,thd->jhd", up_all, keys, preferred_element_type=jnp.float32)
    grad_down = jnp.einsum("htj,thd->jhd", hidden_all, targets, preferred_element_type=jnp.float32)
    return jnp.stack([grad_gate, grad_up, grad_down], axis=2)


def renew(weights, grad_rows, step_size):
    grads = jnp.moveaxis(grad_rows, 0, 1)
    scale = jnp.sqrt(jnp.mean(grads * grads, axis=2, keepdims=True) + 1e-06)
    return weights - step_size[:, None, None] * grads / scale


def local(query_one, key_one, value_one, rate_one, query_two, w_gate, w_up, w_down, step_size):
    heads_local = w_gate.shape[0]
    width = w_gate.shape[2]
    moved = (
        lax.all_to_all(query_one, "head", split_axis=1, concat_axis=0, tiled=True),
        lax.all_to_all(key_one, "head", split_axis=1, concat_axis=0, tiled=True),
        lax.all_to_all(value_one, "head", split_axis=1, concat_axis=0, tiled=True),
        lax.all_to_all(rate_one, "head", split_axis=1, concat_axis=0, tiled=True),
        lax.all_to_all(query_two, "head", split_axis=1, concat_axis=0, tiled=True),
    )
    tokens = moved[0].shape[0]
    query_a = moved[0].reshape(tokens, heads_local, width)
    keys = moved[1].reshape(tokens, heads_local, width)
    values = moved[2].reshape(tokens, heads_local, width)
    rates = moved[3].astype(jnp.float32)
    query_b = moved[4].reshape(tokens, heads_local, width)
    targets = (-(rates[:, :, None] * values.astype(jnp.float32))).astype(jnp.bfloat16)
    pieces = (
        lax.all_gather(w_gate.astype(jnp.bfloat16), "tok", axis=1, tiled=True),
        lax.all_gather(w_up.astype(jnp.bfloat16), "tok", axis=1, tiled=True),
        lax.all_gather(w_down.astype(jnp.bfloat16), "tok", axis=1, tiled=True),
    )
    out_term, grad_gate_pre, grad_up_pre, hidden_k = forward_piece(
        query_a, keys, targets, pieces[0], pieces[1], pieces[2]
    )
    first_block = out_term.reshape(tokens, heads_local * width).astype(jnp.bfloat16)
    grad_local = lax.psum_scatter(
        gradient_rows(grad_gate_pre, grad_up_pre, hidden_k, keys, targets),
        "tok",
        scatter_dimension=0,
        tiled=True,
    )
    gate_new = renew(w_gate, grad_local[:, :, 0, :], step_size)
    up_new = renew(w_up, grad_local[:, :, 1, :], step_size)
    down_new = renew(w_down, grad_local[:, :, 2, :], step_size)
    pieces = (
        lax.all_gather(gate_new.astype(jnp.bfloat16), "tok", axis=1, tiled=True),
        lax.all_gather(up_new.astype(jnp.bfloat16), "tok", axis=1, tiled=True),
        lax.all_gather(down_new.astype(jnp.bfloat16), "tok", axis=1, tiled=True),
    )
    second_total = apply_piece(query_b, pieces[0], pieces[1], pieces[2])
    second_block = second_total.reshape(tokens, heads_local * width).astype(jnp.bfloat16)
    first_back, second_back = (
        lax.all_to_all(first_block, "head", split_axis=0, concat_axis=1, tiled=True),
        lax.all_to_all(second_block, "head", split_axis=0, concat_axis=1, tiled=True),
    )
    return (first_back, second_back, gate_new, up_new, down_new)


def solution(mesh):
    in_specs = (
        P(("head", "tok"), None),
        P(("head", "tok"), None),
        P(("head", "tok"), None),
        P(("head", "tok"), None),
        P(("head", "tok"), None),
        P("head", "tok", None),
        P("head", "tok", None),
        P("head", "tok", None),
        P("head"),
    )
    out_specs = (
        P(("head", "tok"), None),
        P(("head", "tok"), None),
        P("head", "tok", None),
        P("head", "tok", None),
        P("head", "tok", None),
    )
    return jax.shard_map(local, mesh=mesh, in_specs=in_specs, out_specs=out_specs, check_vma=False)
```

profile of v0, /device:TPU:1, one launch (start us, length us, event | category | flops | bytes accessed | tf_op | source)
XLA Modules:
  0.0 1364.1 jit_solution(18135310961557693874)
XLA Ops:
  7.2 1.3 copy.43
  8.4 10.1 all-to-all-start.2
  19.3 76.5 %all_gather.20 = bf16[1,512,512]{2,1,0:T(8,128)(2,1)S(1)} all-gather(bf16[1,8,512]{2,1,0:T(8,128)(2,1)S(1)} %convert_element_type.143), channel_id=1, replica_groups=mesh['head'=8,'tok'=64] {'tok'}, dimensions={1}, use_global_device_ids=true | all-gather | bytes 532480 | tf_op jit(solution)/shard_map/all_gather | solution.py:62
  95.8 0.7 convert_element_type.141
  96.5 73.1 %all_gather.19 = bf16[1,512,512]{2,1,0:T(8,128)(2,1)S(1)} all-gather(bf16[1,8,512]{2,1,0:T(8,128)(2,1)S(1)} %convert_element_type.141), channel_id=1, replica_groups=mesh['head'=8,'tok'=64] {'tok'}, dimensions={1}, use_global_device_ids=true | all-gather | bytes 532480 | tf_op jit(solution)/shard_map/all_gather | solution.py:61
  170.4 1.7 copy.66
  172.0 1.7 copy.65
  173.7 55.9 %all-to-all-start.4 = ((bf16[32,8,512]{2,0,1:T(8,128)(2,1)}), bf16[32,8,512]{2,0,1:T(8,128)(2,1)S(1)}, u32[]{:S(2)}, u32[]{:S(2)}) async-start(bf16[32,8,512]{2,0,1:T(8,128)(2,1)} %bitcast.139), calls=%async_computation.4 | async-start | bytes 524288 | tf_op jit(solution)/shard_map/all_to_all | solution.py:47
  229.7 71.9 %all_gather.18 = bf16[1,512,512]{2,1,0:T(8,128)(2,1)S(1)} all-gather(bf16[1,8,512]{2,1,0:T(8,128)(2,1)S(1)} %convert_element_type.140), channel_id=1, replica_groups=mesh['head'=8,'tok'=64] {'tok'}, dimensions={1}, use_global_device_ids=true | all-gather | bytes 532480 | tf_op jit(solution)/shard_map/all_gather | solution.py:60
  301.7 30.4 %all-to-all-start.3 = ((bf16[32,8,512]{2,0,1:T(8,128)(2,1)}), bf16[32,8,512]{2,0,1:T(8,128)(2,1)S(1)}, u32[]{:S(2)}, u32[]{:S(2)}) async-start(bf16[32,8,512]{2,0,1:T(8,128)(2,1)} %bitcast.140), calls=%async_computation.3 | async-start | bytes 524288 | tf_op jit(solution)/shard_map/all_to_all | solution.py:48
  332.7 5.8 all-to-all-done.3
  340.3 1.9 pad_maximum_fusion
  342.2 0.9 copy-done
  343.2 0.7 copy.67
  343.9 4.4 all-to-all-start
  348.3 0.7 copy.64
  349.7 5.1 all-to-all-done
  354.8 4.4 all-to-all-start.5
  359.5 1.3 convolution_convert_fusion.1
  360.7 665.9 %reduce-scatter.2.cloned.1.call-done = f32[8,1,3,512]{3,0,2,1:T(8,128)} async-done(((f32[512,1,3,512]{3,0,2,1:T(8,128)}), f32[8,1,3,512]{3,0,2,1:T(8,128)}) %reduce-scatter.2.cloned.1.call-update) | async-done | bytes 49168 | tf_op jit(solution)/shard_map/reduce_scatter | solution.py:68
  1026.6 0.9 multiply_reduce_fusion.1
  1027.6 1.5 fusion.47
  1029.0 72.6 %all_gather.23 = bf16[1,512,512]{2,1,0:T(8,128)(2,1)S(1)} all-gather(bf16[1,8,512]{2,1,0:T(8,128)(2,1)S(1)} %get-tuple-element.14), channel_id=1, replica_groups=mesh['head'=8,'tok'=64] {'tok'}, dimensions={1}, use_global_device_ids=true | all-gather | bytes 532480 | tf_op jit(solution)/shard_map/all_gather | solution.py:79
  1101.6 73.4 %all_gather.21 = bf16[1,512,512]{2,1,0:T(8,128)(2,1)S(1)} all-gather(bf16[1,8,512]{2,1,0:T(8,128)(2,1)S(1)} %get-tuple-element.16), channel_id=1, replica_groups=mesh['head'=8,'tok'=64] {'tok'}, dimensions={1}, use_global_device_ids=true | all-gather | bytes 532480 | tf_op jit(solution)/shard_map/all_gather | solution.py:80
  1175.0 72.8 %all_gather.22 = bf16[1,512,512]{2,1,0:T(8,128)(2,1)S(1)} all-gather(bf16[1,8,512]{2,1,0:T(8,128)(2,1)S(1)} %get-tuple-element.8), channel_id=1, replica_groups=mesh['head'=8,'tok'=64] {'tok'}, dimensions={1}, use_global_device_ids=true | all-gather | bytes 532480 | tf_op jit(solution)/shard_map/all_gather | solution.py:78
  1247.8 91.3 %all-to-all-start.1 = ((bf16[8,32,512]{2,1,0:T(8,128)(2,1)}), bf16[8,32,512]{2,1,0:T(8,128)(2,1)S(1)}, u32[]{:S(2)}, u32[]{:S(2)}) async-start(bf16[8,32,512]{2,1,0:T(8,128)(2,1)} %bitcast.9), calls=%async_computation.1 | async-start | bytes 524288 | tf_op jit(solution)/shard_map/all_to_all | solution.py:85
  1339.5 1.3 convolution_convert_fusion
  1340.7 4.9 all-to-all-done.1
  1345.6 4.4 all-to-all-start.6
  1350.0 0.7 copy.58
  1350.7 5.8 all-to-all-done.6
  1356.5 0.7 copy.59
  (30 shorter events, 4.6 us)
Async XLA Ops:
  8.4 165.3 %all-to-all-start.2 = ((bf16[32,8,1]{0,2,1:T(2,128)(2,1)}), bf16[32,8,1]{0,2,1:T(2,128)(2,1)S(1)}, u32[]{:S(2)}, u32[]{:S(2)}) async-start(bf16[32,8,1]{0,2,1:T(2,128)(2,1)} %copy.43), calls=%async_computation.2 | async-start | bytes 8192 | tf_op jit(solution)/shard_map/all_to_all | solution.py:49
  173.7 128.0 %all-to-all-start.4 = ((bf16[32,8,512]{2,0,1:T(8,128)(2,1)}), bf16[32,8,512]{2,0,1:T(8,128)(2,1)S(1)}, u32[]{:S(2)}, u32[]{:S(2)}) async-start(bf16[32,8,512]{2,0,1:T(8,128)(2,1)} %bitcast.139), calls=%async_computation.4 | async-start | bytes 524288 | tf_op jit(solution)/shard_map/all_to_all | solution.py:47
  301.7 36.9 %all-to-all-start.3 = ((bf16[32,8,512]{2,0,1:T(8,128)(2,1)}), bf16[32,8,512]{2,0,1:T(8,128)(2,1)S(1)}, u32[]{:S(2)}, u32[]{:S(2)}) async-start(bf16[32,8,512]{2,0,1:T(8,128)(2,1)} %bitcast.140), calls=%async_computation.3 | async-start | bytes 524288 | tf_op jit(solution)/shard_map/all_to_all | solution.py:48
  332.0 694.6 %reduce-scatter.2.cloned.1.call-start = ((), (), s32[]{:S(2)}) async-start(), calls=%async_computation.8 | async-start | bytes 3194880 | tf_op jit(solution)/shard_map/reduce_scatter | solution.py:68
  342.2 0.9 copy-start
  342.2 6.0 copy-start.1
  343.9 10.9 all-to-all-start
  348.3 679.3 %copy-start.2 = (f32[1,8,512]{2,1,0:T(8,128)S(1)}, f32[1,8,512]{2,1,0:T(8,128)}, u32[]{:S(2)}) copy-start(f32[1,8,512]{2,1,0:T(8,128)} %param.16) | copy-start | bytes 49156
  348.3 679.3 %copy-start.3 = (f32[1,8,512]{2,1,0:T(8,128)S(1)}, f32[1,8,512]{2,1,0:T(8,128)}, u32[]{:S(2)}) copy-start(f32[1,8,512]{2,1,0:T(8,128)} %param.15) | copy-start | bytes 49156
  348.3 679.3 %copy-start.4 = (f32[1,8,512]{2,1,0:T(8,128)S(1)}, f32[1,8,512]{2,1,0:T(8,128)}, u32[]{:S(2)}) copy-start(f32[1,8,512]{2,1,0:T(8,128)} %param.14) | copy-start | bytes 49156
  354.8 893.0 %all-to-all-start.5 = ((bf16[32,8,512]{2,0,1:T(8,128)(2,1)}), bf16[32,8,512]{2,0,1:T(8,128)(2,1)S(1)}, u32[]{:S(2)}, u32[]{:S(2)}) async-start(bf16[32,8,512]{2,0,1:T(8,128)(2,1)} %bitcast.138), calls=%async_computation.6 | async-start | bytes 524288 | tf_op jit(solution)/shard_map/all_to_all | solution.py:50
  1247.8 97.8 %all-to-all-start.1 = ((bf16[8,32,512]{2,1,0:T(8,128)(2,1)}), bf16[8,32,512]{2,1,0:T(8,128)(2,1)S(1)}, u32[]{:S(2)}, u32[]{:S(2)}) async-start(bf16[8,32,512]{2,1,0:T(8,128)(2,1)} %bitcast.9), calls=%async_computation.1 | async-start | bytes 524288 | tf_op jit(solution)/shard_map/all_to_all | solution.py:85
  1345.6 10.9 all-to-all-start.6
Sparse Core Ops, SparseCore 0:
  342.4 684.1 reduce-scatter.1
where the time goes:
time: 1370 us; the launch traced here: 1360 us
  waiting for transfers between devices  688 us (50%)
  blocking collectives  440 us (32%)
  starting transfers between devices  201 us (15%)
  between operations  14.8 us (1%)
    reduce_scatter x1, waiting for transfers between devices, local(): lax.psum_scatter(gradient_rows(grad_gate_pre, grad_up_pre, hidden_k, keys...  666 us
    all_to_all x1, starting transfers between devices, local(): lax.all_to_all(first_block, 'head', split_axis=0, concat_axis=1, tiled=True)  91.3 us
    all_gather x1, blocking collectives, local(): lax.all_gather(w_down.astype(jnp.bfloat16), 'tok', axis=1, tiled=True)  76.5 us
    all_gather x1, blocking collectives, local(): lax.all_gather(down_new.astype(jnp.bfloat16), 'tok', axis=1, tiled=True)  73.4 us
    all_gather x1, blocking collectives, local(): lax.all_gather(w_up.astype(jnp.bfloat16), 'tok', axis=1, tiled=True)  73.1 us
    all_gather x1, blocking collectives, local(): lax.all_gather(gate_new.astype(jnp.bfloat16), 'tok', axis=1, tiled=True)  72.8 us
    all_gather x1, blocking collectives, local(): lax.all_gather(up_new.astype(jnp.bfloat16), 'tok', axis=1, tiled=True)  72.6 us
    all_gather x1, blocking collectives, local(): lax.all_gather(w_gate.astype(jnp.bfloat16), 'tok', axis=1, tiled=True)  71.9 us
  transfers between devices with their start and end apart: 8, of which 5 were waited for; matrix products, arithmetic and copies ran while one was open for 1% of the time, Pallas kernels for 0%

commit v1 on v0

--- a/solution.py
+++ b/solution.py
@@ -2,6 +2,10 @@
 import jax.numpy as jnp
 from jax import lax
 from jax.sharding import PartitionSpec as P
+
+bind_the_scenes = lambda field_in: jnp.concatenate(
+    lax.all_to_all(jnp.stack(lax.axis_size("tok") * [field_in], axis=0), "tok", 0, 0), 1
+)
 
 
 def apply_piece(query, gate_b, up_b, down_b):
@@ -77,7 +81,7 @@
     pieces = (
         lax.all_gather(gate_new.astype(jnp.bfloat16), "tok", axis=1, tiled=True),
         lax.all_gather(up_new.astype(jnp.bfloat16), "tok", axis=1, tiled=True),
-        lax.all_gather(down_new.astype(jnp.bfloat16), "tok", axis=1, tiled=True),
+        bind_the_scenes(down_new.astype(jnp.bfloat16)),
     )
     second_total = apply_piece(query_b, pieces[0], pieces[1], pieces[2])
     second_block = second_total.reshape(tokens, heads_local * width).astype(jnp.bfloat16)

time: 1370 us -> 1310 us (0.956)
  blocking collectives: 440 us -> 387 us
  starting transfers between devices: 201 us -> 187 us
    all_gather x1 -> x0, blocking collectives: 73.4 us -> none  [local(): lax.all_gather(down_new.astype(jnp.bfloat16), 'tok', axis=1, tiled=True)]
    all_to_all x1, starting transfers between devices: 91.3 us -> 54.1 us  [local(): lax.all_to_all(first_block, 'head', split_axis=0, concat_axis=1, tiled=True)]
    all_gather x1, blocking collectives: 72.6 us -> 91.7 us  [local(): lax.all_gather(up_new.astype(jnp.bfloat16), 'tok', axis=1, tiled=True)]
  transfers between devices with their start and end apart: 8 -> 9, of which waited for: 5 -> 5; matrix products, arithmetic and copies ran while one was open for 1% -> 1% of each run, Pallas kernels for 0% -> 0%
where the time goes in v1:
time: 1310 us
  waiting for transfers between devices  699 us (53%)
  blocking collectives  387 us (30%)
  starting transfers between devices  187 us (14%)
  between operations  14.8 us (1%)
    reduce_scatter x1, waiting for transfers between devices, local(): lax.psum_scatter(gradient_rows(grad_gate_pre, grad_up_pre, hidden_k, keys...  677 us
    all_gather x1, blocking collectives, local(): lax.all_gather(up_new.astype(jnp.bfloat16), 'tok', axis=1, tiled=True)  91.7 us
    all_gather x1, blocking collectives, local(): lax.all_gather(w_down.astype(jnp.bfloat16), 'tok', axis=1, tiled=True)  76.5 us
    all_gather x1, blocking collectives, local(): lax.all_gather(gate_new.astype(jnp.bfloat16), 'tok', axis=1, tiled=True)  73.2 us
    all_gather x1, blocking collectives, local(): lax.all_gather(w_up.astype(jnp.bfloat16), 'tok', axis=1, tiled=True)  73.1 us
    all_gather x1, blocking collectives, local(): lax.all_gather(w_gate.astype(jnp.bfloat16), 'tok', axis=1, tiled=True)  71.9 us
    all_to_all x1, starting transfers between devices, local(): lax.all_to_all(key_one, 'head', split_axis=1, concat_axis=0, tiled=True)  55.9 us
    all_to_all x1, starting transfers between devices, local(): lax.all_to_all(first_block, 'head', split_axis=0, concat_axis=1, tiled=True)  54.1 us
  transfers between devices with their start and end apart: 9, of which 5 were waited for; matrix products, arithmetic and copies ran while one was open for 1% of the time, Pallas kernels for 0%

profile of v1, /device:TPU:1, one launch (start us, length us, event | category | flops | bytes accessed | tf_op | source)
XLA Modules:
  0.0 1308.5 jit_solution(12223803940045427696)
XLA Ops:
  7.2 1.3 copy.43
  8.4 10.1 all-to-all-start.2
  19.3 76.5 %all_gather.17 = bf16[1,512,512]{2,1,0:T(8,128)(2,1)S(1)} all-gather(bf16[1,8,512]{2,1,0:T(8,128)(2,1)S(1)} %convert_element_type.145), channel_id=1, replica_groups=mesh['head'=8,'tok'=64] {'tok'}, dimensions={1}, use_global_device_ids=true | all-gather | bytes 532480 | tf_op jit(solution)/shard_map/all_gather | solution.py:66
  96.5 73.1 %all_gather.16 = bf16[1,512,512]{2,1,0:T(8,128)(2,1)S(1)} all-gather(bf16[1,8,512]{2,1,0:T(8,128)(2,1)S(1)} %convert_element_type.143), channel_id=1, replica_groups=mesh['head'=8,'tok'=64] {'tok'}, dimensions={1}, use_global_device_ids=true | all-gather | bytes 532480 | tf_op jit(solution)/shard_map/all_gather | solution.py:65
  170.4 1.7 copy.66
  172.0 1.7 copy.65
  173.7 55.9 %all-to-all-start.4 = ((bf16[32,8,512]{2,0,1:T(8,128)(2,1)}), bf16[32,8,512]{2,0,1:T(8,128)(2,1)S(1)}, u32[]{:S(2)}, u32[]{:S(2)}) async-start(bf16[32,8,512]{2,0,1:T(8,128)(2,1)} %bitcast.141), calls=%async_computation.4 | async-start | bytes 524288 | tf_op jit(solution)/shard_map/all_to_all | solution.py:51
  229.7 71.9 %all_gather.15 = bf16[1,512,512]{2,1,0:T(8,128)(2,1)S(1)} all-gather(bf16[1,8,512]{2,1,0:T(8,128)(2,1)S(1)} %convert_element_type.142), channel_id=1, replica_groups=mesh['head'=8,'tok'=64] {'tok'}, dimensions={1}, use_global_device_ids=true | all-gather | bytes 532480 | tf_op jit(solution)/shard_map/all_gather | solution.py:64
  301.7 30.4 %all-to-all-start.3 = ((bf16[32,8,512]{2,0,1:T(8,128)(2,1)}), bf16[32,8,512]{2,0,1:T(8,128)(2,1)S(1)}, u32[]{:S(2)}, u32[]{:S(2)}) async-start(bf16[32,8,512]{2,0,1:T(8,128)(2,1)} %bitcast.142), calls=%async_computation.3 | async-start | bytes 524288 | tf_op jit(solution)/shard_map/all_to_all | solution.py:52
  332.7 5.8 all-to-all-done.3
  340.3 1.9 pad_maximum_fusion
  342.3 0.9 copy-done
  343.2 0.7 copy.67
  343.9 4.4 all-to-all-start
  348.2 0.7 copy.64
  349.6 677.2 %reduce-scatter.2.cloned.1.call-done = f32[8,1,3,512]{3,0,2,1:T(8,128)} async-done(((f32[512,1,3,512]{3,0,2,1:T(8,128)}), f32[8,1,3,512]{3,0,2,1:T(8,128)}) %reduce-scatter.2.cloned.1.call-update) | async-done | bytes 49168 | tf_op jit(solution)/shard_map/reduce_scatter | solution.py:72
  1026.8 0.9 multiply_reduce_fusion.1
  1027.8 16.2 %all-to-all-start.6 = ((bf16[32,8,512]{2,0,1:T(8,128)(2,1)}), bf16[32,8,512]{2,0,1:T(8,128)(2,1)S(1)}, u32[]{:S(2)}, u32[]{:S(2)}) async-start(bf16[32,8,512]{2,0,1:T(8,128)(2,1)} %bitcast.140), calls=%async_computation.7 | async-start | bytes 524288 | tf_op jit(solution)/shard_map/all_to_all | solution.py:54
  1044.0 1.5 fusion.47
  1045.4 5.0 all-to-all-done.6
  1050.4 0.8 stack.14
  1051.3 11.3 all-to-all-start.5
  1062.9 1.3 convolution_convert_fusion.1
  1064.2 91.7 %all_gather.19 = bf16[1,512,512]{2,1,0:T(8,128)(2,1)S(1)} all-gather(bf16[1,8,512]{2,1,0:T(8,128)(2,1)S(1)} %get-tuple-element.14), channel_id=1, replica_groups=mesh['head'=8,'tok'=64] {'tok'}, dimensions={1}, use_global_device_ids=true | all-gather | bytes 532480 | tf_op jit(solution)/shard_map/all_gather | solution.py:83
  1155.9 73.2 %all_gather.18 = bf16[1,512,512]{2,1,0:T(8,128)(2,1)S(1)} all-gather(bf16[1,8,512]{2,1,0:T(8,128)(2,1)S(1)} %get-tuple-element.8), channel_id=1, replica_groups=mesh['head'=8,'tok'=64] {'tok'}, dimensions={1}, use_global_device_ids=true | all-gather | bytes 532480 | tf_op jit(solution)/shard_map/all_gather | solution.py:82
  1229.5 54.1 %all-to-all-start.1 = ((bf16[8,32,512]{2,1,0:T(8,128)(2,1)}), bf16[8,32,512]{2,1,0:T(8,128)(2,1)S(1)}, u32[]{:S(2)}, u32[]{:S(2)}) async-start(bf16[8,32,512]{2,1,0:T(8,128)(2,1)} %bitcast.9), calls=%async_computation.1 | async-start | bytes 524288 | tf_op jit(solution)/shard_map/all_to_all | solution.py:89
  1283.5 1.3 convolution_convert_fusion
  1284.8 5.3 all-to-all-done.1
  1290.1 4.4 all-to-all-start.7
  1294.4 0.7 copy.58
  1295.1 5.8 all-to-all-done.7
  1300.9 0.7 copy.59
  (32 shorter events, 5.3 us)
Async XLA Ops:
  8.4 165.3 %all-to-all-start.2 = ((bf16[32,8,1]{0,2,1:T(2,128)(2,1)}), bf16[32,8,1]{0,2,1:T(2,128)(2,1)S(1)}, u32[]{:S(2)}, u32[]{:S(2)}) async-start(bf16[32,8,1]{0,2,1:T(2,128)(2,1)} %copy.43), calls=%async_computation.2 | async-start | bytes 8192 | tf_op jit(solution)/shard_map/all_to_all | solution.py:53
  173.7 128.0 %all-to-all-start.4 = ((bf16[32,8,512]{2,0,1:T(8,128)(2,1)}), bf16[32,8,512]{2,0,1:T(8,128)(2,1)S(1)}, u32[]{:S(2)}, u32[]{:S(2)}) async-start(bf16[32,8,512]{2,0,1:T(8,128)(2,1)} %bitcast.141), calls=%async_computation.4 | async-start | bytes 524288 | tf_op jit(solution)/shard_map/all_to_all | solution.py:51
  301.7 36.9 %all-to-all-start.3 = ((bf16[32,8,512]{2,0,1:T(8,128)(2,1)}), bf16[32,8,512]{2,0,1:T(8,128)(2,1)S(1)}, u32[]{:S(2)}, u32[]{:S(2)}) async-start(bf16[32,8,512]{2,0,1:T(8,128)(2,1)} %bitcast.142), calls=%async_computation.3 | async-start | bytes 524288 | tf_op jit(solution)/shard_map/all_to_all | solution.py:52
  332.0 694.8 %reduce-scatter.2.cloned.1.call-start = ((), (), s32[]{:S(2)}) async-start(), calls=%async_computation.9 | async-start | bytes 3194880 | tf_op jit(solution)/shard_map/reduce_scatter | solution.py:72
  342.2 0.9 copy-start
  342.2 6.0 copy-start.1
  342.2 701.7 %copy-start.2 = (f32[1,8,512]{2,1,0:T(8,128)S(1)}, f32[1,8,512]{2,1,0:T(8,128)}, u32[]{:S(2)}) copy-start(f32[1,8,512]{2,1,0:T(8,128)} %param.16) | copy-start | bytes 49156
  342.2 701.7 %copy-start.3 = (f32[1,8,512]{2,1,0:T(8,128)S(1)}, f32[1,8,512]{2,1,0:T(8,128)}, u32[]{:S(2)}) copy-start(f32[1,8,512]{2,1,0:T(8,128)} %param.15) | copy-start | bytes 49156
  342.2 701.7 %copy-start.4 = (f32[1,8,512]{2,1,0:T(8,128)S(1)}, f32[1,8,512]{2,1,0:T(8,128)}, u32[]{:S(2)}) copy-start(f32[1,8,512]{2,1,0:T(8,128)} %param.14) | copy-start | bytes 49156
  343.9 683.9 %all-to-all-start = ((bf16[32,8,512]{2,0,1:T(8,128)(2,1)}), bf16[32,8,512]{2,0,1:T(8,128)(2,1)S(1)}, u32[]{:S(2)}, u32[]{:S(2)}) async-start(bf16[32,8,512]{2,0,1:T(8,128)(2,1)} %bitcast.143), calls=%async_computation | async-start | bytes 524288 | tf_op jit(solution)/shard_map/all_to_all | solution.py:50
  1027.8 22.7 %all-to-all-start.6 = ((bf16[32,8,512]{2,0,1:T(8,128)(2,1)}), bf16[32,8,512]{2,0,1:T(8,128)(2,1)S(1)}, u32[]{:S(2)}, u32[]{:S(2)}) async-start(bf16[32,8,512]{2,0,1:T(8,128)(2,1)} %bitcast.140), calls=%async_computation.7 | async-start | bytes 524288 | tf_op jit(solution)/shard_map/all_to_all | solution.py:54
  1051.3 178.2 %all-to-all-start.5 = ((bf16[64,1,8,512]{3,2,1,0:T(8,128)(2,1)}), bf16[64,1,8,512]{3,2,1,0:T(8,128)(2,1)S(1)}, u32[]{:S(2)}, u32[]{:S(2)}) async-start(bf16[64,1,8,512]{3,2,1,0:T(8,128)(2,1)} %stack.14), calls=%async_computation.6 | async-start | bytes 1048576 | tf_op jit(solution)/shard_map/all_to_all | solution.py:7
  1229.5 60.6 %all-to-all-start.1 = ((bf16[8,32,512]{2,1,0:T(8,128)(2,1)}), bf16[8,32,512]{2,1,0:T(8,128)(2,1)S(1)}, u32[]{:S(2)}, u32[]{:S(2)}) async-start(bf16[8,32,512]{2,1,0:T(8,128)(2,1)} %bitcast.9), calls=%async_computation.1 | async-start | bytes 524288 | tf_op jit(solution)/shard_map/all_to_all | solution.py:89
  1290.1 10.9 all-to-all-start.7
Sparse Core Ops, SparseCore 0:
  342.4 684.4 reduce-scatter.1
